TPU v7x, 32 devices: a whole 2x2x4 slice. The times are simulated.
32 devices in a mesh: gx: 2 (over x), gy: 4 (over y, core), gz: 4 (over z).
Axes of the slice: x: 2, y: 2, z: 4, core: 2. Of those that a mesh axis runs over, the one named last changes fastest.
Arguments:
- positions: float32 [3, 16384], P(None, ('gx', 'gy', 'gz')), may hold values from 0 to 1
- features: bfloat16 [64, 16384], P(None, ('gx', 'gy', 'gz')), may hold values from -6 to 6
- species: int32 [16384], P(('gx', 'gy', 'gz')), may hold values from 0 to 3
- species_scale: bfloat16 [4], replicated, may hold values from 0.5 to 2
- w_first: bfloat16 [64, 64], replicated, may hold values from -0.75 to 0.75
- w_second: bfloat16 [64, 64], replicated, may hold values from -0.75 to 0.75
- w_radial: float32 [64, 8], replicated, may hold values from -4 to 4
- w_mid: bfloat16 [64, 64], replicated, may hold values from -0.75 to 0.75
- w_last: bfloat16 [64, 64], replicated, may hold values from -0.75 to 0.75
- w_out: float32 [64], replicated, may hold values from -0.75 to 0.75
- ghost_send: int32 [8192], P(('gx', 'gy', 'gz')), may hold values from 0 to 511
- local_first: int32 [655360], P(('gx', 'gy', 'gz')), may hold values from 0 to 511
- local_second: int32 [655360], P(('gx', 'gy', 'gz')), may hold values from 0 to 511
- local_mask: int32 [655360], P(('gx', 'gy', 'gz')), may hold values 0 or 1
- ghost_owner: int32 [393216], P(('gx', 'gy', 'gz')), may hold values from 0 to 511
- ghost_index: int32 [393216], P(('gx', 'gy', 'gz')), may hold values from 0 to 1791
- ghost_mask: int32 [393216], P(('gx', 'gy', 'gz')), may hold values 0 or 1
Outputs:
- forces: float32 [3, 16384], P(None, ('gx', 'gy', 'gz'))
- atom_energy: float32 [16384], P(('gx', 'gy', 'gz'))
Inputs may be any that keep to these rules, and one draw needn't show every extreme that they name: `ghost_send`: rows of the domain's own atoms. `local_first`: owned atoms of the domain. `local_second`: owned atoms of the domain. `ghost_owner`: owned atoms of the domain. `ghost_index`: ghost rows of the domain.
All inputs are finite; a program needn't handle non-finite values. No bound on the sum of `local_mask` or of `ghost_mask` on one device may be relied on, other than what follows from the above.
Results may differ from a plain program's by a relative error of at most 0.0085.
Values may be sent and summed in bfloat16 or wider, within the bound.
No kernel may reach another device: no remote copies, remote signals or barrier semaphores. Data moves between devices by JAX's collectives and lax.ppermute only.
A program may use at most 64 MiB of HBM per device.

v0:
```python
import functools
import math

import jax
import jax.numpy as jnp
from jax import lax
from jax.experimental import pallas as pl
from jax.experimental.pallas import tpu as pltpu
from jax.sharding import PartitionSpec as P

basis_width = 24.0
domain_edge = 1.0
ghost_offsets = ((1, 0, 0), (0, 1, 0), (0, 0, 1), (1, 1, 0), (1, 0, 1), (0, 1, 1), (1, 1, 1))

PLANAR = ((1, 0), (0, 1), (1, 1))
EXTRA = 8
OFFERED = 16
GROUP = 256
LANES = 128
CHUNK = 256
QUAD = 4
VMEM_LIMIT = 48 * 1024 * 1024

NT = (((1,), (1,)), ((), ()))
f32 = jnp.float32
bf16 = jnp.bfloat16


def dot(left, right):
    return jnp.dot(left, right, preferred_element_type=f32)


def dot_nt(left, right):
    return lax.dot_general(left, right, NT, preferred_element_type=f32)


def iota(shape, dim):
    return lax.broadcasted_iota(jnp.int32, shape, dim)


def one_hot(entry, codes):
    entry = entry.astype(f32)
    entry = jnp.concatenate([entry, entry], 0).astype(bf16)
    entry = jnp.concatenate([entry] * (codes.shape[0] // 16), 0)
    pieces = [
        jnp.where(codes == entry[:, start : start + LANES], bf16(1), bf16(0))
        for start in range(0, entry.shape[1], LANES)
    ]
    return jnp.concatenate(pieces, 1)


def row_codes(count):
    return iota((count, LANES), 0).astype(f32).astype(bf16)


def split_two(value):
    high = value.astype(bf16).astype(f32)
    return high, value - high


def coord_rows(coords, gain):
    high, low = split_two(coords)
    return jnp.concatenate([high, gain, low, jnp.zeros_like(gain)], 0)


def eye(count):
    return (iota((count, count), 0) == iota((count, count), 1)).astype(bf16)


def fetch(sources, targets, landed):
    copies = [
        pltpu.make_async_copy(source, target, landed.at[place])
        for place, (source, target) in enumerate(zip(sources, targets))
    ]
    for copy in copies:
        copy.start()
    for copy in copies:
        copy.wait()


def tables_kernel(*refs):
    own_ref, right_ref, offered_ref, mats_ref, radial_ref, radial_t_ref, out_ref, list_ref, need_ref = refs[14:23]
    send_ref = refs[23]
    landing = refs[24:37]
    fetch(refs[:14], landing + (send_ref,), refs[37])
    positions_ref, features_ref, species_ref, scale_ref, w_first_ref, w_second_ref = landing[:6]
    radial_w_ref, w_mid_ref, w_last_ref, w_out_ref, first_ref, second_ref, mask_ref = landing[6:]
    channels = features_ref.shape[0]
    count = features_ref.shape[1]
    species = species_ref[...]
    gain = jnp.zeros((1, count), f32)
    for kind in range(scale_ref.shape[1]):
        scale = scale_ref[:, kind : kind + 1].astype(f32)
        gain = jnp.where(species == kind, scale, gain)
    positions = positions_ref[...]
    left = dot(w_first_ref[...], features_ref[...]).astype(bf16).astype(f32)
    right = dot(w_second_ref[...], features_ref[...]).astype(bf16).astype(f32)
    own_ref[0:channels, :] = 0.5 * left
    own_ref[channels:, :] = jnp.concatenate([positions, gain, positions, gain], 0)
    column = jnp.concatenate([0.5 * right, coord_rows(positions, gain)], 0)
    groups = count // GROUP
    rows = channels + EXTRA
    table = jnp.concatenate([column[:, group * GROUP : (group + 1) * GROUP] for group in range(groups)], 0)
    spare = right_ref.shape[0] - groups * rows
    if spare:
        table = jnp.concatenate([table, jnp.zeros((spare, GROUP), f32)], 0)
    table = table.astype(bf16)
    right_ref[...] = table
    send = jnp.broadcast_to(send_ref[...], (8, send_ref.shape[1]))
    picked = dot(table, one_hot(send & (GROUP - 1), row_codes(GROUP)))
    chosen = group_pick(picked, send // GROUP, rows, groups)
    chosen = jnp.concatenate([chosen, jnp.zeros((OFFERED - EXTRA, chosen.shape[1]), f32)], 0)
    offered_ref[...] = chosen.astype(bf16)

    unit = eye(channels)
    w_mid = w_mid_ref[...]
    w_last = w_last_ref[...]
    last_t = dot_nt(unit, w_last).astype(bf16)
    mid_t = dot_nt(unit, w_mid).astype(bf16)
    wide = QUAD * channels
    for place, matrix in enumerate((w_mid, w_last, last_t, mid_t)):
        mats_ref[place * wide : (place + 1) * wide, :] = (0.5 * diagonal_copies(matrix)).astype(bf16)
    bases = radial_w_ref.shape[0]
    high, low = split_two(radial_w_ref[...])
    high = high.astype(bf16)
    low = low.astype(bf16)
    spread = dot_nt(unit, jnp.concatenate([high, high, low, low], 0)).astype(bf16)
    radial_ref[...] = (0.5 * diagonal_copies(spread)).astype(bf16)
    radial_t_ref[...] = diagonal_copies(jnp.concatenate([high, low], 0)).astype(bf16)
    w_out = w_out_ref[...]
    diagonal = jnp.where(iota((channels, channels), 0) == iota((channels, channels), 1), w_out, 0.0)
    out_ref[...] = jnp.broadcast_to(jnp.sum(diagonal, axis=1, keepdims=True), (channels, LANES))
    bits = (count - 1).bit_length()
    codes = pack(first_ref[...], second_ref[...], mask_ref[...], bits)
    live = [codes[start : start + 8] & 1 for start in range(0, codes.shape[0], 8)]
    need_ref[...] = gather_live(codes, live, 2 * bits + 1, list_ref)


def pack(owner, partner, mask, partner_bits):
    return (owner * 2**partner_bits + partner) * 2 + mask


def gather_live(codes, live, bits, list_ref):
    tiles = len(live)
    sub = iota((8, LANES), 0)
    passed = jnp.zeros((8, LANES), jnp.int32)
    words = []
    for tile in range(tiles):
        dead = 1 - live[tile]
        for step in (1, 2, 4):
            dead = dead + jnp.where(sub >= step, pltpu.roll(dead, step, 0), 0)
        move = (passed + dead) * 2**bits + codes[tile * 8 : tile * 8 + 8]
        words.append(jnp.where(live[tile] != 0, move, 0))
        passed = passed + jnp.broadcast_to(dead[7:8], (8, LANES))
    none = jnp.zeros((8, LANES), jnp.int32)
    for power in range((tiles * 8).bit_length()):
        step = 2**power
        moving = [jnp.where((word & 2 ** (bits + power)) != 0, word, 0) for word in words]
        if step < 8:
            rolled = [pltpu.roll(word, 8 - step, 0) for word in moving] + [none]
            come = [jnp.where(sub < 8 - step, rolled[tile], rolled[tile + 1]) for tile in range(tiles)]
        else:
            come = (moving[step // 8 :] + [none] * tiles)[:tiles]
        words = [word - gone + new for word, gone, new in zip(words, moving, come)]
    for tile, word in enumerate(words):
        list_ref[tile * 8 : tile * 8 + 8, :] = word & (2**bits - 1)
    return tiles * 8 - passed


def diagonal_copies(matrix):
    high, wide = matrix.shape
    repeat = (iota((wide, QUAD * wide), 0) == iota((wide, QUAD * wide), 1) % wide).astype(bf16)
    row = dot(matrix, repeat)
    full = jnp.concatenate([row] * QUAD, 0)
    return jnp.where(iota(full.shape, 0) // high == iota(full.shape, 1) // wide, full, 0.0)


def group_pick(values, high, rows, groups):
    high = jnp.concatenate([high] * (rows // 8), 0)
    chosen = values[:rows]
    for group in range(1, groups):
        chosen = jnp.where(high == group, values[group * rows : (group + 1) * rows], chosen)
    return chosen


def spread_groups(values, high, groups):
    second = iota(values.shape, 0) // 4
    pieces = [jnp.where(high == second + group, values, 0.0) for group in range(0, groups, 2)]
    return jnp.concatenate(pieces, 0)


def lane_pick(table_ref, place, first=0):
    rows, count = table_ref.shape[0] - first, table_ref.shape[1]
    lane = jnp.concatenate([place & (LANES - 1)] * (rows // 8), 0)
    high = jnp.concatenate([place // LANES] * (rows // 8), 0)
    chosen = None
    for group in range(count // LANES):
        part = table_ref[first:, group * LANES : (group + 1) * LANES]
        picked = jnp.take_along_axis(part, lane, axis=1, mode="promise_in_bounds")
        chosen = picked if chosen is None else jnp.where(high == group, picked, chosen)
    return chosen


def sum_rows(values, steps):
    for step in steps:
        values = values + pltpu.roll(values, step, 0)
    return values


def pair_tasks(
    own_groups,
    partner_groups,
    channels,
    bases,
    list_ref,
    own_ref,
    right_ref,
    mats_ref,
    radial_ref,
    radial_t_ref,
    out_ref,
    sums,
    hot,
    hot_wide,
    slope_one,
    slope_two,
    codes_ref,
):
    rows = channels + EXTRA
    line = CHUNK // LANES
    block = QUAD * line
    wide = QUAD * channels
    w_out = jnp.concatenate([out_ref[...]] * line, 1)
    centers = iota((bases, CHUNK), 0).astype(f32) * (1.0 / (bases - 1))
    last = iota((8, CHUNK), 0) % 4 == 3
    partner_bits = (partner_groups * LANES - 1).bit_length()
    quads = range(QUAD)
    codes_ref[...] = row_codes(GROUP)

    def matrix(place):
        return mats_ref[place * wide : (place + 1) * wide, :]

    def part(values, number, size=channels):
        return values[number * size : (number + 1) * size]

    def silu_pair(half):
        grow = jnp.tanh(half)
        plus = 1.0 + grow
        hidden = half * plus
        return hidden, plus + hidden * (1.0 - grow)

    def task(first, number):
        at = pl.multiple_of(first * block, block)
        code_rows = list_ref[pl.ds(at, block), :]
        owners, partners, lives, projected, shifts, squares, weights, stacks, slopes = ([] for _ in range(9))
        for quad in quads:
            cols = slice(quad * CHUNK, (quad + 1) * CHUNK)
            code = jnp.concatenate(
                [
                    jnp.broadcast_to(code_rows[row : row + 1, :], (8, LANES))
                    for row in range(quad * line, (quad + 1) * line)
                ],
                1,
            )
            lives.append((code & 1).astype(f32))
            partner = (code >> 1) & (2**partner_bits - 1)
            owner = code >> (partner_bits + 1)
            owners.append(owner)
            partners.append(partner)
            hot[number, 0:LANES, cols] = one_hot(owner & (LANES - 1), codes_ref[0:LANES, :])
            wide = one_hot(partner & (GROUP - 1), codes_ref[...])
            hot_wide[number, :, cols] = wide
            hot[number, LANES:, cols] = wide[0:LANES] + wide[LANES:]
            yield
        for quad in quads:
            cols = slice(quad * CHUNK, (quad + 1) * CHUNK)
            own_vals = jnp.concatenate(
                [lane_pick(own_ref, owners[quad][:, start : start + LANES]) for start in range(0, CHUNK, LANES)], 1
            )
            partner_vals = group_pick(
                dot(right_ref[...], hot_wide[number, :, cols]),
                partners[quad] // GROUP,
                rows,
                partner_groups * LANES // GROUP,
            )
            projected.append(own_vals[:channels] + partner_vals[:channels])
            own_coords = own_vals[channels:]
            extra = partner_vals[channels:]
            partner_coords = extra + pltpu.roll(extra, 4, 0)
            shift = partner_coords - own_coords
            squared = sum_rows(jnp.where(last, 0.0, shift * shift), (2, 1))
            gain = sum_rows(jnp.where(last, own_coords * partner_coords, 0.0), (2, 1))
            weights.append(lives[quad] * gain)
            away = squared - centers
            basis = jnp.exp(-basis_width * (away * away))
            basis_high, basis_low = split_two(basis)
            stacks.append(jnp.concatenate([basis_high, basis_low, basis_high, basis_low], 0).astype(bf16))
            slopes.append((-2.0 * basis_width) * away * basis)
            shifts.append(shift)
            squares.append(squared)
            yield
        radial = dot(radial_ref[...], jnp.concatenate(stacks, 0))
        yield
        pieces = []
        for quad in quads:
            hidden, slope_one[number, quad] = silu_pair(projected[quad] + part(radial, quad))
            pieces.append(hidden.astype(bf16))
        yield
        half = dot(matrix(0), jnp.concatenate(pieces, 0))
        yield
        pieces = []
        for quad in quads:
            hidden, slope_two[number, quad] = silu_pair(part(half, quad))
            pieces.append(hidden.astype(bf16))
        yield
        half = dot(matrix(1), jnp.concatenate(pieces, 0))
        yield
        pieces = []
        readouts = []
        for quad in quads:
            hidden, slope = silu_pair(part(half, quad))
            terms = w_out * hidden
            terms = sum(terms[start : start + 8] for start in range(8, channels, 8)) + terms[:8]
            readouts.append(sum_rows(terms, (4, 2, 1)))
            pieces.append(((0.5 * w_out) * slope).astype(bf16))
        yield
        back = dot(matrix(2), jnp.concatenate(pieces, 0))
        yield
        pieces = [(part(back, quad) * slope_two[number, quad]).astype(bf16) for quad in quads]
        back = dot(matrix(3), jnp.concatenate(pieces, 0))
        yield
        pieces = [(part(back, quad) * slope_one[number, quad]).astype(bf16) for quad in quads]
        back = dot(radial_t_ref[...], jnp.concatenate(pieces, 0))
        yield
        parts = []
        for quad in quads:
            two = part(back, quad, 2 * bases)
            readout_slope = sum_rows((two[:bases] + two[bases:]) * slopes[quad], (4, 2, 1))
            near = jnp.maximum(1.0 - squares[quad], 0.0)
            weight_near = weights[quad] * near
            energy = weight_near * near * readouts[quad]
            slope = weight_near * (near * readout_slope - 2.0 * readouts[quad])
            push = (2.0 * slope) * shifts[quad]
            values = jnp.where(last, energy, push)
            parts.append(
                jnp.concatenate(
                    [
                        spread_groups(values, owners[quad] // LANES, own_groups),
                        spread_groups(values, partners[quad] // LANES, partner_groups),
                    ],
                    0,
                ).astype(bf16)
            )
        yield
        sums[...] += dot_nt(jnp.concatenate(parts, 1), hot[number])

    return task


def run(tasks, then=None, later=()):
    running, waiting = [], list(tasks)
    while running or waiting or then is not None:
        if waiting:
            running.append(waiting.pop(0))
        if then is not None and next(then, then) is then:
            then = None
            waiting += later
        for _ in range(2):
            running = [task for task in running if next(task, task) is not task]


def run_rest(task, done, rest):
    steps, size = rest

    def step(index, unused):
        run([task(done + index * size + number, number) for number in range(size)])
        return unused

    lax.fori_loop(0, steps, step, 0)


def rest_of(need, done, total):
    left = total - done
    size = 2 if left % 2 == 0 else 1
    rows = QUAD * CHUNK // LANES
    return jnp.maximum(need - done * rows + size * rows - 1, 0) // (size * rows), size


def local_kernel(channels, bases, first_quad, quad_count, counts, *refs):
    count = 7 + sum(counts)
    codes, own, right, *weights = refs[:7]
    sums, hot, *scratch = refs[count:]
    sums[...] = refs[7][...] if counts[0] else jnp.zeros_like(sums)
    groups = own.shape[1] // LANES
    task = pair_tasks(groups, groups, channels, bases, codes, own, right, *weights, sums, hot, *scratch)
    run([task(first_quad + number, number) for number in range(quad_count)])
    if counts[1]:
        done = first_quad + quad_count
        need = jnp.max(refs[7 + counts[0]][...])
        run_rest(task, done, rest_of(need, done, codes.shape[0] * LANES // (QUAD * CHUNK)))


def near_ones(codes, bits, own_ref, channels, coords_ref, found):
    sub = iota((8, LANES), 0)
    for start in range(0, codes.shape[0], 8):
        tile = codes[start : start + 8]
        squared = jnp.zeros((8, LANES), f32)
        for low in range(4):
            code = jnp.where(
                sub < 4,
                jnp.broadcast_to(tile[low : low + 1], (8, LANES)),
                jnp.broadcast_to(tile[low + 4 : low + 5], (8, LANES)),
            )
            shift = lane_pick(coords_ref, (code >> 1) & (2**bits - 1)) - lane_pick(own_ref, code >> (bits + 1), channels)
            square = shift * shift
            total = square + pltpu.roll(square, 7, 0) + pltpu.roll(square, 6, 0)
            if low:
                total = pltpu.roll(total, low, 0)
            squared = jnp.where(sub % 4 == low, total, squared)
        found.append(jnp.where(squared < 1.001, tile & 1, 0))
        yield


def ghost_kernel(quad_count, local_quads, channels, bases, *refs):
    blocks = len(ghost_offsets)
    owner, partner, mask, own, *weights = refs[:8]
    local, right, sums_in = refs[8:11]
    arrived = refs[11 : 12 + len(PLANAR)]
    sums_out, upward, *level = refs[12 + len(PLANAR) : 14 + 2 * len(PLANAR)]
    table, sums, codes_ref, coords_ref, *scratch = refs[14 + 2 * len(PLANAR) :]
    half = len(scratch) // 2
    groups = own.shape[1] // LANES
    partner_groups = blocks * GROUP // LANES
    sums[...] = jnp.zeros_like(sums)
    pieces = []
    for offset in ghost_offsets:
        if offset[:2] == (0, 0):
            source, start = arrived[0], 0
        else:
            source, start = arrived[1 + PLANAR.index(offset[:2])], offset[2] * (channels + OFFERED)
        extra = source[start + channels : start + channels + OFFERED, :].astype(f32)
        moved = jnp.concatenate(
            [extra[axis : axis + 1] + extra[axis + 4 : axis + 5] + domain_edge * offset[axis] for axis in range(3)], 0
        )
        pieces += [source[start : start + channels, :].astype(f32), coord_rows(moved, extra[3:4])]
        place = ghost_offsets.index(offset) * GROUP
        coords_ref[:, place : place + GROUP] = jnp.concatenate([moved, extra[3:4], moved, extra[3:4]], 0)
    pieces.append(jnp.zeros((table.shape[0] - blocks * (channels + EXTRA), GROUP), f32))
    table[...] = jnp.concatenate(pieces, 0).astype(bf16)
    bits = (partner_groups * LANES - 1).bit_length()
    codes = pack(owner[...], partner[...], mask[...], bits)
    sums_out[...] = sums_in[...]
    local_task = pair_tasks(
        groups, groups, channels, bases, local, own, right, *weights, sums_out, *scratch[:half]
    )
    task = pair_tasks(
        groups, partner_groups, channels, bases, codes_ref, own, table, *weights, sums, *scratch[half:]
    )
    need = []

    def search():
        live = []
        yield from near_ones(codes, bits, own, channels, coords_ref, live)
        need.append(gather_live(codes, live, bits + (own.shape[1] - 1).bit_length() + 1, codes_ref))
        yield

    run(
        [local_task(quad, quad - local_quads[0]) for quad in range(*local_quads)],
        search(),
        [task(number, number) for number in range(quad_count)],
    )
    total = owner.shape[0] * LANES // (QUAD * CHUNK)
    run_rest(task, quad_count, rest_of(jnp.max(need[0]), quad_count, total))
    first = groups * 4
    sums_out[0:first, :] += sums[0:first, :]
    for block, offset in enumerate(ghost_offsets):
        halves = []
        for half in range(GROUP // LANES):
            start = first + (block * (GROUP // LANES) + half) * 4
            halves.append(sums[start : start + 4, LANES:])
        force = -jnp.concatenate(halves, 1)
        force = jnp.concatenate([force, jnp.zeros_like(force)], 0)
        if offset[2]:
            place = 0 if offset[:2] == (0, 0) else 1 + PLANAR.index(offset[:2])
            upward[place * 8 : place * 8 + 8, :] = force
        else:
            level[PLANAR.index(offset[:2])][...] = force


def pair_kernel(offered_ref, from_z_ref, unused_ref, both_ref):
    count = offered_ref.shape[0]
    both_ref[0:count, :] = offered_ref[...]
    both_ref[count:, :] = from_z_ref[...]


def merge_kernel(*refs):
    upward, *level = refs[: 1 + len(PLANAR)]
    outs = refs[2 + len(PLANAR) :]
    outs[0][...] = upward[0:8, :]
    for place, part in enumerate(level):
        outs[1 + place][...] = part[...] + upward[8 * place + 8 : 8 * place + 16, :]


def final_kernel(*refs):
    sums_ref, send_ref, *arrived = refs[:-2]
    forces_ref, energy_ref = refs[-2:]
    incoming = arrived[0][...]
    for part in arrived[1:]:
        incoming = incoming + part[...]
    high, low = split_two(jnp.concatenate([incoming[:4], incoming[:4]], 0))
    send = jnp.broadcast_to(send_ref[...], (8, send_ref.shape[1]))
    groups = sums_ref.shape[0] // 8
    hot = one_hot(send & (LANES - 1), row_codes(LANES))
    spread = [spread_groups(value, send // LANES, groups).astype(bf16) for value in (high, low)]
    back = dot_nt(jnp.concatenate(spread, 0), hot)
    back = back[: groups * 4] + back[groups * 4 :]
    for group in range(groups):
        own = sums_ref[group * 4 : group * 4 + 4, 0:LANES]
        partner = sums_ref[(groups + group) * 4 : (groups + group) * 4 + 4, LANES:]
        total = own - partner + back[group * 4 : group * 4 + 4]
        cols = slice(group * LANES, (group + 1) * LANES)
        forces_ref[:, cols] = total[0:3]
        energy_ref[:, cols] = own[3:4]


def whole(shape, dtype):
    return jax.ShapeDtypeStruct(shape, dtype)


def call(kernel, outs, name, scratch=(), specs=None, cost=None):
    more = {} if cost is None else dict(cost_estimate=cost)
    return pl.pallas_call(
        kernel,
        grid=(1,),
        in_specs=specs,
        out_specs=tuple(pl.BlockSpec(memory_space=pltpu.VMEM) for _ in outs),
        out_shape=outs,
        scratch_shapes=list(scratch),
        compiler_params=pltpu.CompilerParams(vmem_limit_bytes=VMEM_LIMIT),
        name=name,
        **more,
    )


def shifted(value, offset, sizes, sign):
    used = tuple(axis for axis, step in zip(sizes, offset) if step)
    dims = [size for name, size in used]
    pairs = []
    for flat in range(math.prod(dims)):
        place, rest = [], flat
        for size in reversed(dims):
            place.insert(0, rest % size)
            rest //= size
        target = 0
        for at, size in zip(place, dims):
            target = target * size + (at - sign) % size
        pairs.append((flat, target))
    return lax.ppermute(value, tuple(name for name, size in used), pairs)


def on_device(
    sizes,
    positions,
    features,
    species,
    species_scale,
    w_first,
    w_second,
    w_radial,
    w_mid,
    w_last,
    w_out,
    ghost_send,
    local_first,
    local_second,
    local_mask,
    ghost_owner,
    ghost_index,
    ghost_mask,
):
    channels, own_count = features.shape
    send_count = ghost_send.shape[0]
    bases = w_radial.shape[1]
    rows = channels + EXTRA
    groups = own_count // LANES
    blocks = len(ghost_offsets)
    whole_spec = pl.BlockSpec(memory_space=pltpu.VMEM)
    def tiles(value):
        return value.reshape(value.shape[0] // LANES, LANES)

    def fetching(kernel, name, outs, operands, kept):
        here = [pltpu.with_memory_space_constraint(value, pltpu.HBM) for value in operands]
        landing = operands[: len(operands) - kept]
        return call(
            kernel,
            outs + tuple(whole(value.shape, value.dtype) for value in operands[len(landing) :]),
            name,
            [pltpu.VMEM(value.shape, value.dtype) for value in landing]
            + [pltpu.SemaphoreType.DMA((len(operands),))],
            [pl.BlockSpec(memory_space=pltpu.HBM)] * len(operands),
        )(*here)

    own, right, offered, *weights, local, need, send = fetching(
        tables_kernel,
        "tables",
        (
            whole((rows, own_count), f32),
            whole((-(-own_count // GROUP * rows // 16) * 16, GROUP), bf16),
            whole((channels + OFFERED, send_count), bf16),
            whole((4 * QUAD * channels, QUAD * channels), bf16),
            whole((QUAD * channels, QUAD * 4 * bases), bf16),
            whole((QUAD * 2 * bases, QUAD * channels), bf16),
            whole((channels, LANES), f32),
            whole((local_first.shape[0] // LANES, LANES), jnp.int32),
            whole((8, LANES), jnp.int32),
        ),
        (
            positions,
            features,
            species.reshape(1, own_count),
            species_scale.reshape(1, species_scale.shape[0]),
            w_first,
            w_second,
            w_radial.T,
            w_mid,
            w_last,
            w_out.reshape(1, channels),
            tiles(local_first),
            tiles(local_second),
            tiles(local_mask),
            ghost_send.reshape(1, send_count),
        ),
        1,
    )
    from_z = shifted(offered, (0, 0, 1), sizes, 1)

    def scratch(per_step, hots):
        return [pltpu.VMEM((per_step, GROUP, QUAD * CHUNK), bf16) for _ in range(hots)] + [
            pltpu.VMEM((per_step, QUAD, channels, CHUNK), f32),
            pltpu.VMEM((per_step, QUAD, channels, CHUNK), f32),
            pltpu.VMEM((GROUP, LANES), bf16),
        ]

    def cost(slots):
        return pl.CostEstimate(flops=slots * 400000, bytes_accessed=slots * 12, transcendentals=slots * 200)

    quads = local.shape[0] * LANES // (QUAD * CHUNK)
    cuts = [(0, quads // 4), (quads // 4, quads * 2 // 5), (quads * 3 // 5, quads * 4 // 5), (quads * 4 // 5, quads * 9 // 10)]
    beside = (cuts[1][1], cuts[2][0])

    def local_call(part, start, needed, after):
        operands = [local, own, right, *weights, *start, *needed, *after]
        first, end = cuts[part]
        size = end - first
        (sums,) = call(
            functools.partial(
                local_kernel, channels, bases, first, size, (len(start), len(needed), len(after))
            ),
            (whole((groups * 8, GROUP), f32),),
            "local_pairs",
            scratch(size, 2),
            [whole_spec] * len(operands),
            cost(size * QUAD * CHUNK),
        )(*operands)
        return sums

    sums = local_call(0, (), (), ())
    (both,) = call(
        pair_kernel, (whole((2 * offered.shape[0], send_count), bf16),), "two_blocks", specs=[whole_spec] * 3
    )(offered, from_z, sums)
    arrived = [from_z] + [shifted(both, (*step, 0), sizes, 1) for step in PLANAR]
    sums = local_call(1, (sums,), (), (both,))
    ghost_lists = [tiles(value) for value in (ghost_owner, ghost_index, ghost_mask)]
    ghost_step = ghost_owner.shape[0] // (QUAD * CHUNK) // 3
    partner_rows = blocks * GROUP // LANES * 4
    table_rows = -(-blocks * rows // 16) * 16
    force = whole((8, send_count), f32)
    sums, upward, *level = call(
        functools.partial(ghost_kernel, ghost_step, beside, channels, bases),
        (whole((groups * 8, GROUP), f32), whole((8 + 8 * len(PLANAR), send_count), f32)) + (force,) * len(PLANAR),
        "ghost_pairs",
        [
            pltpu.VMEM((table_rows, GROUP), bf16),
            pltpu.VMEM((groups * 4 + partner_rows, GROUP), f32),
            pltpu.VMEM((ghost_owner.shape[0] // LANES, LANES), jnp.int32),
            pltpu.VMEM((8, blocks * GROUP), f32),
        ]
        + scratch(beside[1] - beside[0], 2)
        + scratch(ghost_step, 2),
        [whole_spec] * (11 + len(arrived)),
        cost(ghost_owner.shape[0]),
    )(*ghost_lists, own, *weights, local, right, sums, *arrived)
    upward = shifted(upward, (0, 0, 1), sizes, -1)
    sums = local_call(2, (sums,), (), ())
    mine, *level = call(
        merge_kernel, (force,) * (1 + len(PLANAR)), "forces_upward", specs=[whole_spec] * (2 + len(PLANAR))
    )(upward, *level, sums)
    returned = [shifted(part, (*step, 0), sizes, -1) for part, step in zip(level, PLANAR)]
    sums = local_call(3, (sums,), (need,), (mine,))
    forces, energy = call(
        final_kernel,
        (whole((3, own_count), f32), whole((1, own_count), f32)),
        "totals",
        specs=[whole_spec] * (3 + len(returned)),
    )(sums, send, mine, *returned)
    return forces, energy.reshape(own_count)


def solution(mesh):
    names = ("gx", "gy", "gz")
    sizes = tuple((name, mesh.shape[name]) for name in names)
    split = P(names)
    cols = P(None, names)
    in_specs = (cols, cols, split) + (P(),) * 7 + (split,) * 7
    return jax.shard_map(
        functools.partial(on_device, sizes),
        mesh=mesh,
        in_specs=in_specs,
        out_specs=(cols, split),
        check_vma=False,
    )
```

profile of v0, /device:TPU:0, one launch (start us, length us, event | category | flops | bytes accessed | tf_op | source)
XLA Modules:
  0.0 41.1 jit_solution(15027619040227398464)
XLA Ops:
  0.6 1.9 %tables.1 = (f32[72,512]{1,0:T(8,128)S(1)}, bf16[144,256]{1,0:T(8,128)(2,1)S(1)}, bf16[80,256]{1,0:T(8,128)(2,1)S(1)}, bf16[1024,256]{1,0:T(8,128)(2,1)S(1)}, bf...) custom-call(f32[3,512]{1,0:T(4,128)} %refs_0_.1, ...), custom_call_target="tpu_custom_call" | custom-call | tf_op jit(solution)/shard_map/tables/pallas_call | solution.py:594
  2.5 5.1 %collective-permute-start = (bf16[80,256]{1,0:T(8,128)(2,1)S(1)}, bf16[80,256]{1,0:T(8,128)(2,1)S(1)}, u32[]{:S(2)}, u32[]{:S(2)}) collective-permute-start(bf16[80,256]{1,0:T(8,128)(2,1)S(1)} %get-tuple-element.30.offered_ref), channel_id=1, source_target_pairs={{0,3},{1,0},{2,1},{3,2},{4,7},{5,4},{6,5},{7,6},{8,11},{9,8},{10,9... | collective-permute-start | bytes 122888 | tf_op jit(solution)/shard_map/ppermute | solution.py:558
  7.6 4.9 %local_pairs.4.unused_ref.refs_7_ = f32[32,256]{1,0:T(8,128)S(1)} custom-call(s32[160,128]{1,0:T(8,128)S(1)} %get-tuple-element.23.refs_0_.refs_8_, f32[72,512]{1,0:T(8,128)S(1)} %get-tuple-element.24.refs_1_.refs_3_, bf16[144,256]{1,0:T(8,128)(2,1)S(1)} %get-tuple-element.25.refs_2_.refs_9_, bf16[1024,256]{1,0:T(8,128)(2,1)S(1)} %get-tuple-element.26.refs_3_.refs_4_, ...), custom_call_target="tpu_custom_call" | custom-call | flops 2048000000 | bytes 61440 | tf_op jit(solution)/shard_map/local_pairs/pallas_call | solution.py:655
  12.5 0.0 collective-permute-done.from_z_ref.refs_11_
  12.6 0.0 copy-start
  12.6 0.0 copy-start.1
  12.6 0.0 copy-start.2
  12.6 1.7 %collective-permute-start.3 = (bf16[160,256]{1,0:T(8,128)(2,1)S(1)}, bf16[160,256]{1,0:T(8,128)(2,1)S(1)}, u32[]{:S(2)}, u32[]{:S(2)}) collective-permute-start(bf16[160,256]{1,0:T(8,128)(2,1)S(1)} %two_blocks.1.refs_8_), channel_id=1, source_target_pairs={{0,28},{4,16},{8,20},{12,24},{16,12},{20,0},{24,4},{28,8},{1,29},{... | collective-permute-start | bytes 245768 | tf_op jit(solution)/shard_map/ppermute | solution.py:558
  14.3 1.1 %collective-permute-start.2 = (bf16[160,256]{1,0:T(8,128)(2,1)S(1)}, bf16[160,256]{1,0:T(8,128)(2,1)S(1)}, u32[]{:S(2)}, u32[]{:S(2)}) collective-permute-start(bf16[160,256]{1,0:T(8,128)(2,1)S(1)} %two_blocks.1.refs_8_), channel_id=1, source_target_pairs={{0,12},{4,0},{8,4},{12,8},{1,13},{5,1},{9,5},{13,9},{2,14},{6,2},{... | collective-permute-start | bytes 245768 | tf_op jit(solution)/shard_map/ppermute | solution.py:558
  15.4 0.5 %collective-permute-start.1 = (bf16[160,256]{1,0:T(8,128)(2,1)S(1)}, bf16[160,256]{1,0:T(8,128)(2,1)S(1)}, u32[]{:S(2)}, u32[]{:S(2)}) collective-permute-start(bf16[160,256]{1,0:T(8,128)(2,1)S(1)} %two_blocks.1.refs_8_), channel_id=1, source_target_pairs={{0,16},{16,0},{1,17},{17,1},{2,18},{18,2},{3,19},{19,3},{4,20},{20... | collective-permute-start | bytes 245768 | tf_op jit(solution)/shard_map/ppermute | solution.py:558
  15.9 3.4 %local_pairs.5.refs_10_ = f32[32,256]{1,0:T(8,128)S(1)} custom-call(s32[160,128]{1,0:T(8,128)S(1)} %get-tuple-element.23.refs_0_.refs_8_, f32[72,512]{1,0:T(8,128)S(1)} %get-tuple-element.24.refs_1_.refs_3_, bf16[144,256]{1,0:T(8,128)(2,1)S(1)} %get-tuple-element.25.refs_2_.refs_9_, bf16[1024,256]{1,0:T(8,128)(2,1)S(1)} %get-tuple-element.26.refs_3_.refs_4_, ...), custom_call_target="tpu_custom_call" | custom-call | flops 1228800000 | bytes 36864 | tf_op jit(solution)/shard_map/local_pairs/pallas_call | solution.py:655
  19.4 0.0 collective-permute-done.3.refs_14_
  19.4 0.0 collective-permute-done.2.refs_13_
  19.4 0.4 %collective-permute-done.1.refs_12_ = bf16[160,256]{1,0:T(8,128)(2,1)S(1)} collective-permute-done((bf16[160,256]{1,0:T(8,128)(2,1)S(1)}, bf16[160,256]{1,0:T(8,128)(2,1)S(1)}, u32[]{:S(2)}, u32[]{:S(2)}) %collective-permute-start.1) | collective-permute-done | bytes 81952 | tf_op jit(solution)/shard_map/ppermute | solution.py:558
  19.8 0.0 copy-done
  19.8 0.0 copy-done.1
  19.8 0.0 copy-done.2
  19.9 9.4 %ghost_pairs.1 = (f32[32,256]{1,0:T(8,128)S(1)}, f32[32,256]{1,0:T(8,128)S(1)}, f32[8,256]{1,0:T(8,128)S(1)}, f32[8,256]{1,0:T(8,128)S(1)}, f32[8,256]{1,0:T(8,128)S(1)}) custom-call(s32[96,128]{1,0:T(8,128)S(1)} %bitcast.12, s32[96,128]{1,0:T(8,128)S(1)} %bitcast.13, s32[96,128]{1,0:T(8,128)S(1)} %bitcast.14, ...), custom_call_target="tpu_custom_call" | custom-call | flops 4915200000 | bytes 147456 | tf_op jit(solution)/shard_map/ghost_pairs/pallas_call | solution.py:678
  29.3 0.1 collective-permute-start.4
  29.3 4.2 %local_pairs.6.refs_4_.refs_7_ = f32[32,256]{1,0:T(8,128)S(1)} custom-call(s32[160,128]{1,0:T(8,128)S(1)} %get-tuple-element.23.refs_0_.refs_8_, f32[72,512]{1,0:T(8,128)S(1)} %get-tuple-element.24.refs_1_.refs_3_, bf16[144,256]{1,0:T(8,128)(2,1)S(1)} %get-tuple-element.25.refs_2_.refs_9_, bf16[1024,256]{1,0:T(8,128)(2,1)S(1)} %get-tuple-element.26.refs_3_.refs_4_, ...), custom_call_target="tpu_custom_call" | custom-call | flops 1638400000 | bytes 49152 | tf_op jit(solution)/shard_map/local_pairs/pallas_call | solution.py:655
  33.6 1.5 %collective-permute-done.4.refs_0_ = f32[32,256]{1,0:T(8,128)S(1)} collective-permute-done((f32[32,256]{1,0:T(8,128)S(1)}, f32[32,256]{1,0:T(8,128)S(1)}, u32[]{:S(2)}, u32[]{:S(2)}) %collective-permute-start.4) | collective-permute-done | bytes 32800 | tf_op jit(solution)/shard_map/ppermute | solution.py:558
  35.1 1.1 %collective-permute-start.5 = (f32[8,256]{1,0:T(8,128)S(1)}, f32[8,256]{1,0:T(8,128)S(1)}, u32[]{:S(2)}, u32[]{:S(2)}) collective-permute-start(f32[8,256]{1,0:T(8,128)S(1)} %get-tuple-element.39), channel_id=1, source_target_pairs={{0,16},{16,0},{1,17},{17,1},{2,18},{18,2},{3,19},{19,3},{4,20},{20... | collective-permute-start | bytes 24584 | tf_op jit(solution)/shard_map/ppermute | solution.py:558
  36.1 0.0 collective-permute-start.6
  36.1 1.5 %collective-permute-start.7 = (f32[8,256]{1,0:T(8,128)S(1)}, f32[8,256]{1,0:T(8,128)S(1)}, u32[]{:S(2)}, u32[]{:S(2)}) collective-permute-start(f32[8,256]{1,0:T(8,128)S(1)} %get-tuple-element.41), channel_id=1, source_target_pairs={{0,20},{4,24},{8,28},{12,16},{16,4},{20,8},{24,12},{28,0},{1,21},{... | collective-permute-start | bytes 24584 | tf_op jit(solution)/shard_map/ppermute | solution.py:558
  37.6 2.7 %local_pairs.7.refs_0_ = f32[32,256]{1,0:T(8,128)S(1)} custom-call(s32[160,128]{1,0:T(8,128)S(1)} %get-tuple-element.23.refs_0_.refs_8_, f32[72,512]{1,0:T(8,128)S(1)} %get-tuple-element.24.refs_1_.refs_3_, bf16[144,256]{1,0:T(8,128)(2,1)S(1)} %get-tuple-element.25.refs_2_.refs_9_, bf16[1024,256]{1,0:T(8,128)(2,1)S(1)} %get-tuple-element.26.refs_3_.refs_4_, ...), custom_call_target="tpu_custom_call" | custom-call | flops 819200000 | bytes 24576 | tf_op jit(solution)/shard_map/local_pairs/pallas_call | solution.py:655
  40.3 0.0 collective-permute-done.5.refs_3_
  40.4 0.0 collective-permute-done.6.refs_4_
  40.4 0.0 collective-permute-done.7.refs_5_
  40.4 0.8 %totals.1 = (f32[3,512]{1,0:T(4,128)}, f32[1,512]{1,0:T(1,128)}) custom-call(f32[32,256]{1,0:T(8,128)S(1)} %local_pairs.7.refs_0_, s32[1,256]{1,0:T(1,128)S(1)} %get-tuple-element.38.refs_1_, f32[8,256]{1,0:T(8,128)S(1)} %get-tuple-element.37.refs_9_.refs_2_, f32[8,256]{1,0:T(8,128)S(1)} %collective-permute-done.5.refs_3_, ...), custom_call_target="tpu_custom_call" | custom-call | tf_op jit(solution)/shard_map/totals/pallas_call | solution.py:700
  (2 shorter events, 0.0 us)
Async XLA Ops:
  2.5 10.0 %collective-permute-start = (bf16[80,256]{1,0:T(8,128)(2,1)S(1)}, bf16[80,256]{1,0:T(8,128)(2,1)S(1)}, u32[]{:S(2)}, u32[]{:S(2)}) collective-permute-start(bf16[80,256]{1,0:T(8,128)(2,1)S(1)} %get-tuple-element.30.offered_ref), channel_id=1, source_target_pairs={{0,3},{1,0},{2,1},{3,2},{4,7},{5,4},{6,5},{7,6},{8,11},{9,8},{10,9... | collective-permute-start | bytes 122888 | tf_op jit(solution)/shard_map/ppermute | solution.py:558
  12.6 7.3 %copy-start = (s32[12288]{0:T(1024)S(1)}, s32[12288]{0:T(1024)}, u32[]{:S(2)}) copy-start(s32[12288]{0:T(1024)} %param.31) | copy-start | bytes 147460
  12.6 7.3 %copy-start.1 = (s32[12288]{0:T(1024)S(1)}, s32[12288]{0:T(1024)}, u32[]{:S(2)}) copy-start(s32[12288]{0:T(1024)} %param.32) | copy-start | bytes 147460
  12.6 7.3 %copy-start.2 = (s32[12288]{0:T(1024)S(1)}, s32[12288]{0:T(1024)}, u32[]{:S(2)}) copy-start(s32[12288]{0:T(1024)} %param.33) | copy-start | bytes 147460
  12.6 6.8 %collective-permute-start.3 = (bf16[160,256]{1,0:T(8,128)(2,1)S(1)}, bf16[160,256]{1,0:T(8,128)(2,1)S(1)}, u32[]{:S(2)}, u32[]{:S(2)}) collective-permute-start(bf16[160,256]{1,0:T(8,128)(2,1)S(1)} %two_blocks.1.refs_8_), channel_id=1, source_target_pairs={{0,28},{4,16},{8,20},{12,24},{16,12},{20,0},{24,4},{28,8},{1,29},{... | collective-permute-start | bytes 245768 | tf_op jit(solution)/shard_map/ppermute | solution.py:558
  14.3 5.1 %collective-permute-start.2 = (bf16[160,256]{1,0:T(8,128)(2,1)S(1)}, bf16[160,256]{1,0:T(8,128)(2,1)S(1)}, u32[]{:S(2)}, u32[]{:S(2)}) collective-permute-start(bf16[160,256]{1,0:T(8,128)(2,1)S(1)} %two_blocks.1.refs_8_), channel_id=1, source_target_pairs={{0,12},{4,0},{8,4},{12,8},{1,13},{5,1},{9,5},{13,9},{2,14},{6,2},{... | collective-permute-start | bytes 245768 | tf_op jit(solution)/shard_map/ppermute | solution.py:558
  15.4 4.4 %collective-permute-start.1 = (bf16[160,256]{1,0:T(8,128)(2,1)S(1)}, bf16[160,256]{1,0:T(8,128)(2,1)S(1)}, u32[]{:S(2)}, u32[]{:S(2)}) collective-permute-start(bf16[160,256]{1,0:T(8,128)(2,1)S(1)} %two_blocks.1.refs_8_), channel_id=1, source_target_pairs={{0,16},{16,0},{1,17},{17,1},{2,18},{18,2},{3,19},{19,3},{4,20},{20... | collective-permute-start | bytes 245768 | tf_op jit(solution)/shard_map/ppermute | solution.py:558
  29.3 5.8 %collective-permute-start.4 = (f32[32,256]{1,0:T(8,128)S(1)}, f32[32,256]{1,0:T(8,128)S(1)}, u32[]{:S(2)}, u32[]{:S(2)}) collective-permute-start(f32[32,256]{1,0:T(8,128)S(1)} %get-tuple-element.33), channel_id=1, source_target_pairs={{0,1},{1,2},{2,3},{3,0},{4,5},{5,6},{6,7},{7,4},{8,9},{9,10},{10,1... | collective-permute-start | bytes 98312 | tf_op jit(solution)/shard_map/ppermute | solution.py:558
  35.1 5.3 %collective-permute-start.5 = (f32[8,256]{1,0:T(8,128)S(1)}, f32[8,256]{1,0:T(8,128)S(1)}, u32[]{:S(2)}, u32[]{:S(2)}) collective-permute-start(f32[8,256]{1,0:T(8,128)S(1)} %get-tuple-element.39), channel_id=1, source_target_pairs={{0,16},{16,0},{1,17},{17,1},{2,18},{18,2},{3,19},{19,3},{4,20},{20... | collective-permute-start | bytes 24584 | tf_op jit(solution)/shard_map/ppermute | solution.py:558
  36.1 4.2 %collective-permute-start.6 = (f32[8,256]{1,0:T(8,128)S(1)}, f32[8,256]{1,0:T(8,128)S(1)}, u32[]{:S(2)}, u32[]{:S(2)}) collective-permute-start(f32[8,256]{1,0:T(8,128)S(1)} %get-tuple-element.40), channel_id=1, source_target_pairs={{0,4},{4,8},{8,12},{12,0},{1,5},{5,9},{9,13},{13,1},{2,6},{6,10},{... | collective-permute-start | bytes 24584 | tf_op jit(solution)/shard_map/ppermute | solution.py:558
  36.1 4.2 %collective-permute-start.7 = (f32[8,256]{1,0:T(8,128)S(1)}, f32[8,256]{1,0:T(8,128)S(1)}, u32[]{:S(2)}, u32[]{:S(2)}) collective-permute-start(f32[8,256]{1,0:T(8,128)S(1)} %get-tuple-element.41), channel_id=1, source_target_pairs={{0,20},{4,24},{8,28},{12,16},{16,4},{20,8},{24,12},{28,0},{1,21},{... | collective-permute-start | bytes 24584 | tf_op jit(solution)/shard_map/ppermute | solution.py:558
where the time goes:
time: 41.3 us; the launch traced here: 41.1 us
  Pallas kernels  27.4 us (66%)
  starting transfers between devices  11.1 us (27%)
  waiting for transfers between devices  1.97 us (5%)
  between operations  0.74 us (2%)
    pallas_call x4, Pallas kernels, local_call(): call(functools.partial(local_kernel, channels, bases, first, size, (len(s...  15.3 us
    ppermute x8, starting transfers between devices, shifted(): return lax.ppermute(value, tuple((name for name, size in used)), pairs)  11.1 us
    pallas_call x1, Pallas kernels, on_device(): call(functools.partial(ghost_kernel, ghost_step, beside, channels, bases)...  9.43 us
    ppermute x8, waiting for transfers between devices, shifted(): return lax.ppermute(value, tuple((name for name, size in used)), pairs)  1.97 us
    pallas_call x1, Pallas kernels, fetching(): call(kernel, outs + tuple((whole(value.shape, value.dtype) for value in o...  1.87 us
  transfers between devices with their start and end apart: 8, of which 2 were waited for; matrix products, arithmetic and copies ran while one was open for 0% of the time, Pallas kernels for 37%

commit v1 on v0

--- a/solution.py
+++ b/solution.py
@@ -357,14 +357,11 @@
     return task
 
 
-def run(tasks, then=None, later=()):
+def run(tasks):
     running, waiting = [], list(tasks)
-    while running or waiting or then is not None:
+    while running or waiting:
         if waiting:
             running.append(waiting.pop(0))
-        if then is not None and next(then, then) is then:
-            then = None
-            waiting += later
         for _ in range(2):
             running = [task for task in running if next(task, task) is not task]
 
@@ -379,11 +376,29 @@
     lax.fori_loop(0, steps, step, 0)
 
 
-def rest_of(need, done, total):
+def fold(list_ref, source, target, turns):
+    rows = slice(target * 8, target * 8 + 8)
+    spare = slice(source * 8, source * 8 + 8)
+    kept = list_ref[rows, :]
+    moving = pltpu.roll(list_ref[spare, :], 4, 0)
+    for turn in range(turns):
+        moving = pltpu.roll(moving, 1, 1)
+        if turn % 4 == 3:
+            moving = pltpu.roll(moving, 3, 0)
+        placed = jnp.where(kept == 0, moving, 0)
+        kept = kept + placed
+        moving = moving - placed
+    list_ref[rows, :] = kept
+    list_ref[spare, :] = moving
+
+
+def rest_of(list_ref, need, done, total):
     left = total - done
-    size = 2 if left % 2 == 0 else 1
+    size = next(size for size in (3, 2, 1) if left % size == 0)
     rows = QUAD * CHUNK // LANES
-    return jnp.maximum(need - done * rows + size * rows - 1, 0) // (size * rows), size
+    found = jnp.max(list_ref[done * rows : total * rows, :])
+    steps = jnp.maximum(jnp.max(need) - done * rows + size * rows - 1, 0) // (size * rows)
+    return jnp.where(found > 0, steps, 0), size
 
 
 def local_kernel(channels, bases, first_quad, quad_count, counts, *refs):
@@ -392,16 +407,24 @@
     sums, hot, *scratch = refs[count:]
     sums[...] = refs[7][...] if counts[0] else jnp.zeros_like(sums)
     groups = own.shape[1] // LANES
+    if counts[1]:
+        tail, *scratch = scratch
+        tile = QUAD * CHUNK // LANES // 8
+        tail[...] = codes[...]
+        fold(tail, (first_quad + quad_count) * tile, (first_quad + quad_count) * tile - 1, 12)
+        fold(tail, (first_quad + quad_count) * tile + 1, (first_quad + quad_count) * tile - 1, 8)
+        codes = tail
     task = pair_tasks(groups, groups, channels, bases, codes, own, right, *weights, sums, hot, *scratch)
     run([task(first_quad + number, number) for number in range(quad_count)])
     if counts[1]:
         done = first_quad + quad_count
-        need = jnp.max(refs[7 + counts[0]][...])
-        run_rest(task, done, rest_of(need, done, codes.shape[0] * LANES // (QUAD * CHUNK)))
-
-
-def near_ones(codes, bits, own_ref, channels, coords_ref, found):
+        total = codes.shape[0] * LANES // (QUAD * CHUNK)
+        run_rest(task, done, rest_of(codes, refs[7 + counts[0]][...], done, total))
+
+
+def near_ones(codes, bits, own_ref, channels, coords_ref):
     sub = iota((8, LANES), 0)
+    found = []
     for start in range(0, codes.shape[0], 8):
         tile = codes[start : start + 8]
         squared = jnp.zeros((8, LANES), f32)
@@ -418,17 +441,16 @@
                 total = pltpu.roll(total, low, 0)
             squared = jnp.where(sub % 4 == low, total, squared)
         found.append(jnp.where(squared < 1.001, tile & 1, 0))
-        yield
-
-
-def ghost_kernel(quad_count, local_quads, channels, bases, *refs):
+    return found
+
+
+def ghost_kernel(quad_count, channels, bases, *refs):
     blocks = len(ghost_offsets)
     owner, partner, mask, own, *weights = refs[:8]
-    local, right, sums_in = refs[8:11]
-    arrived = refs[11 : 12 + len(PLANAR)]
-    sums_out, upward, *level = refs[12 + len(PLANAR) : 14 + 2 * len(PLANAR)]
-    table, sums, codes_ref, coords_ref, *scratch = refs[14 + 2 * len(PLANAR) :]
-    half = len(scratch) // 2
+    sums_in = refs[8]
+    arrived = refs[9 : 10 + len(PLANAR)]
+    sums_out, upward, *level = refs[10 + len(PLANAR) : 12 + 2 * len(PLANAR)]
+    table, sums, codes_ref, coords_ref, *scratch = refs[12 + 2 * len(PLANAR) :]
     groups = own.shape[1] // LANES
     partner_groups = blocks * GROUP // LANES
     sums[...] = jnp.zeros_like(sums)
@@ -449,30 +471,17 @@
     table[...] = jnp.concatenate(pieces, 0).astype(bf16)
     bits = (partner_groups * LANES - 1).bit_length()
     codes = pack(owner[...], partner[...], mask[...], bits)
-    sums_out[...] = sums_in[...]
-    local_task = pair_tasks(
-        groups, groups, channels, bases, local, own, right, *weights, sums_out, *scratch[:half]
-    )
-    task = pair_tasks(
-        groups, partner_groups, channels, bases, codes_ref, own, table, *weights, sums, *scratch[half:]
-    )
-    need = []
-
-    def search():
-        live = []
-        yield from near_ones(codes, bits, own, channels, coords_ref, live)
-        need.append(gather_live(codes, live, bits + (own.shape[1] - 1).bit_length() + 1, codes_ref))
-        yield
-
-    run(
-        [local_task(quad, quad - local_quads[0]) for quad in range(*local_quads)],
-        search(),
-        [task(number, number) for number in range(quad_count)],
-    )
+    live = near_ones(codes, bits, own, channels, coords_ref)
+    need = gather_live(codes, live, bits + (own.shape[1] - 1).bit_length() + 1, codes_ref)
+    tile = quad_count * QUAD * CHUNK // LANES // 8
+    fold(codes_ref, tile, tile - 1, 8)
+    task = pair_tasks(groups, partner_groups, channels, bases, codes_ref, own, table, *weights, sums, *scratch)
+    run([task(number, number) for number in range(quad_count)])
     total = owner.shape[0] * LANES // (QUAD * CHUNK)
-    run_rest(task, quad_count, rest_of(jnp.max(need[0]), quad_count, total))
+    run_rest(task, quad_count, rest_of(codes_ref, need, quad_count, total))
     first = groups * 4
-    sums_out[0:first, :] += sums[0:first, :]
+    sums_out[0:first, :] = sums_in[0:first, :] + sums[0:first, :]
+    sums_out[first:, :] = sums_in[first:, :]
     for block, offset in enumerate(ghost_offsets):
         halves = []
         for half in range(GROUP // LANES):
@@ -634,8 +643,9 @@
     )
     from_z = shifted(offered, (0, 0, 1), sizes, 1)
 
-    def scratch(per_step, hots):
-        return [pltpu.VMEM((per_step, GROUP, QUAD * CHUNK), bf16) for _ in range(hots)] + [
+    def scratch(per_step, hots, more=()):
+        hot = [pltpu.VMEM((per_step, GROUP, QUAD * CHUNK), bf16) for _ in range(hots)]
+        return hot[:1] + list(more) + hot[1:] + [
             pltpu.VMEM((per_step, QUAD, channels, CHUNK), f32),
             pltpu.VMEM((per_step, QUAD, channels, CHUNK), f32),
             pltpu.VMEM((GROUP, LANES), bf16),
@@ -645,20 +655,19 @@
         return pl.CostEstimate(flops=slots * 400000, bytes_accessed=slots * 12, transcendentals=slots * 200)
 
     quads = local.shape[0] * LANES // (QUAD * CHUNK)
-    cuts = [(0, quads // 4), (quads // 4, quads * 2 // 5), (quads * 3 // 5, quads * 4 // 5), (quads * 4 // 5, quads * 9 // 10)]
-    beside = (cuts[1][1], cuts[2][0])
+    cuts = [0, quads // 4, quads * 2 // 5, quads * 13 // 20, quads * 4 // 5]
 
     def local_call(part, start, needed, after):
         operands = [local, own, right, *weights, *start, *needed, *after]
-        first, end = cuts[part]
-        size = end - first
+        first = cuts[part]
+        size = cuts[part + 1] - first
         (sums,) = call(
             functools.partial(
                 local_kernel, channels, bases, first, size, (len(start), len(needed), len(after))
             ),
             (whole((groups * 8, GROUP), f32),),
             "local_pairs",
-            scratch(size, 2),
+            scratch(size, 2, [pltpu.VMEM(local.shape, local.dtype)] if needed else []),
             [whole_spec] * len(operands),
             cost(size * QUAD * CHUNK),
         )(*operands)
@@ -671,12 +680,12 @@
     arrived = [from_z] + [shifted(both, (*step, 0), sizes, 1) for step in PLANAR]
     sums = local_call(1, (sums,), (), (both,))
     ghost_lists = [tiles(value) for value in (ghost_owner, ghost_index, ghost_mask)]
-    ghost_step = ghost_owner.shape[0] // (QUAD * CHUNK) // 3
+    ghost_step = ghost_owner.shape[0] // (QUAD * CHUNK) // 4
     partner_rows = blocks * GROUP // LANES * 4
     table_rows = -(-blocks * rows // 16) * 16
     force = whole((8, send_count), f32)
     sums, upward, *level = call(
-        functools.partial(ghost_kernel, ghost_step, beside, channels, bases),
+        functools.partial(ghost_kernel, ghost_step, channels, bases),
         (whole((groups * 8, GROUP), f32), whole((8 + 8 * len(PLANAR), send_count), f32)) + (force,) * len(PLANAR),
         "ghost_pairs",
         [
@@ -685,11 +694,10 @@
             pltpu.VMEM((ghost_owner.shape[0] // LANES, LANES), jnp.int32),
             pltpu.VMEM((8, blocks * GROUP), f32),
         ]
-        + scratch(beside[1] - beside[0], 2)
         + scratch(ghost_step, 2),
-        [whole_spec] * (11 + len(arrived)),
+        [whole_spec] * (9 + len(arrived)),
         cost(ghost_owner.shape[0]),
-    )(*ghost_lists, own, *weights, local, right, sums, *arrived)
+    )(*ghost_lists, own, *weights, sums, *arrived)
     upward = shifted(upward, (0, 0, 1), sizes, -1)
     sums = local_call(2, (sums,), (), ())
     mine, *level = call(

time: 41.3 us -> 40 us (0.969)
  Pallas kernels: 27.4 us -> 26.3 us
  waiting for transfers between devices: 1.97 us -> 1.27 us
    pallas_call x1, Pallas kernels: 9.43 us -> 6 us  [on_device(): call(functools.partial(ghost_kernel, ghost_step, channels, bases), (whole...]
    pallas_call x4, Pallas kernels: 15.3 us -> 17.6 us  [local_call(): call(functools.partial(local_kernel, channels, bases, first, size, (len(s...]
    ppermute x8, waiting for transfers between devices: 1.97 us -> 1.27 us  [shifted(): return lax.ppermute(value, tuple((name for name, size in used)), pairs)]
  transfers between devices with their start and end apart: 8 -> 8, of which waited for: 2 -> 2; matrix products, arithmetic and copies ran while one was open for 0% -> 0% of each run, Pallas kernels for 37% -> 44%
where the time goes in v1:
time: 40 us; the launch traced here: 39.6 us
  Pallas kernels  26.3 us (66%)
  starting transfers between devices  11.3 us (28%)
  waiting for transfers between devices  1.27 us (3%)
  between operations  0.74 us (2%)
    pallas_call x4, Pallas kernels, local_call(): call(functools.partial(local_kernel, channels, bases, first, size, (len(s...  17.6 us
    ppermute x8, starting transfers between devices, shifted(): return lax.ppermute(value, tuple((name for name, size in used)), pairs)  11.3 us
    pallas_call x1, Pallas kernels, on_device(): call(functools.partial(ghost_kernel, ghost_step, channels, bases), (whole...  6 us
    pallas_call x1, Pallas kernels, fetching(): call(kernel, outs + tuple((whole(value.shape, value.dtype) for value in o...  1.87 us
    ppermute x8, waiting for transfers between devices, shifted(): return lax.ppermute(value, tuple((name for name, size in used)), pairs)  1.27 us
  transfers between devices with their start and end apart: 8, of which 2 were waited for; matrix products, arithmetic and copies ran while one was open for 0% of the time, Pallas kernels for 44%

profile of v1, /device:TPU:0, one launch (start us, length us, event | category | flops | bytes accessed | tf_op | source)
XLA Modules:
  0.0 39.6 jit_solution(7464753288131156539)
XLA Ops:
  0.6 1.9 %tables.1 = (f32[72,512]{1,0:T(8,128)S(1)}, bf16[144,256]{1,0:T(8,128)(2,1)S(1)}, bf16[80,256]{1,0:T(8,128)(2,1)S(1)}, bf16[1024,256]{1,0:T(8,128)(2,1)S(1)}, bf...) custom-call(f32[3,512]{1,0:T(4,128)} %refs_0_.1, ...), custom_call_target="tpu_custom_call" | custom-call | tf_op jit(solution)/shard_map/tables/pallas_call | solution.py:603
  2.5 5.1 %collective-permute-start = (bf16[80,256]{1,0:T(8,128)(2,1)S(1)}, bf16[80,256]{1,0:T(8,128)(2,1)S(1)}, u32[]{:S(2)}, u32[]{:S(2)}) collective-permute-start(bf16[80,256]{1,0:T(8,128)(2,1)S(1)} %get-tuple-element.30.offered_ref), channel_id=1, source_target_pairs={{0,3},{1,0},{2,1},{3,2},{4,7},{5,4},{6,5},{7,6},{8,11},{9,8},{10,9... | collective-permute-start | bytes 122888 | tf_op jit(solution)/shard_map/ppermute | solution.py:567
  7.6 4.9 %local_pairs.4.unused_ref.refs_7_ = f32[32,256]{1,0:T(8,128)S(1)} custom-call(s32[160,128]{1,0:T(8,128)S(1)} %get-tuple-element.23.refs_0_, f32[72,512]{1,0:T(8,128)S(1)} %get-tuple-element.24.refs_1_.refs_3_, bf16[144,256]{1,0:T(8,128)(2,1)S(1)} %get-tuple-element.25.refs_2_, bf16[1024,256]{1,0:T(8,128)(2,1)S(1)} %get-tuple-element.26.refs_3_.refs_4_, ...), custom_call_target="tpu_custom_call" | custom-call | flops 2048000000 | bytes 61440 | tf_op jit(solution)/shard_map/local_pairs/pallas_call | solution.py:664
  12.5 0.0 collective-permute-done.from_z_ref.refs_9_
  12.6 0.0 copy-start
  12.6 0.0 copy-start.1
  12.6 0.0 copy-start.2
  12.6 1.7 %collective-permute-start.3 = (bf16[160,256]{1,0:T(8,128)(2,1)S(1)}, bf16[160,256]{1,0:T(8,128)(2,1)S(1)}, u32[]{:S(2)}, u32[]{:S(2)}) collective-permute-start(bf16[160,256]{1,0:T(8,128)(2,1)S(1)} %two_blocks.1.refs_8_), channel_id=1, source_target_pairs={{0,28},{4,16},{8,20},{12,24},{16,12},{20,0},{24,4},{28,8},{1,29},{... | collective-permute-start | bytes 245768 | tf_op jit(solution)/shard_map/ppermute | solution.py:567
  14.3 1.1 %collective-permute-start.2 = (bf16[160,256]{1,0:T(8,128)(2,1)S(1)}, bf16[160,256]{1,0:T(8,128)(2,1)S(1)}, u32[]{:S(2)}, u32[]{:S(2)}) collective-permute-start(bf16[160,256]{1,0:T(8,128)(2,1)S(1)} %two_blocks.1.refs_8_), channel_id=1, source_target_pairs={{0,12},{4,0},{8,4},{12,8},{1,13},{5,1},{9,5},{13,9},{2,14},{6,2},{... | collective-permute-start | bytes 245768 | tf_op jit(solution)/shard_map/ppermute | solution.py:567
  15.4 0.5 %collective-permute-start.1 = (bf16[160,256]{1,0:T(8,128)(2,1)S(1)}, bf16[160,256]{1,0:T(8,128)(2,1)S(1)}, u32[]{:S(2)}, u32[]{:S(2)}) collective-permute-start(bf16[160,256]{1,0:T(8,128)(2,1)S(1)} %two_blocks.1.refs_8_), channel_id=1, source_target_pairs={{0,16},{16,0},{1,17},{17,1},{2,18},{18,2},{3,19},{19,3},{4,20},{20... | collective-permute-start | bytes 245768 | tf_op jit(solution)/shard_map/ppermute | solution.py:567
  15.9 3.4 %local_pairs.5.refs_8_ = f32[32,256]{1,0:T(8,128)S(1)} custom-call(s32[160,128]{1,0:T(8,128)S(1)} %get-tuple-element.23.refs_0_, f32[72,512]{1,0:T(8,128)S(1)} %get-tuple-element.24.refs_1_.refs_3_, bf16[144,256]{1,0:T(8,128)(2,1)S(1)} %get-tuple-element.25.refs_2_, bf16[1024,256]{1,0:T(8,128)(2,1)S(1)} %get-tuple-element.26.refs_3_.refs_4_, ...), custom_call_target="tpu_custom_call" | custom-call | flops 1228800000 | bytes 36864 | tf_op jit(solution)/shard_map/local_pairs/pallas_call | solution.py:664
  19.4 0.0 collective-permute-done.3.refs_12_
  19.4 0.0 collective-permute-done.2.refs_11_
  19.4 0.4 %collective-permute-done.1.refs_10_ = bf16[160,256]{1,0:T(8,128)(2,1)S(1)} collective-permute-done((bf16[160,256]{1,0:T(8,128)(2,1)S(1)}, bf16[160,256]{1,0:T(8,128)(2,1)S(1)}, u32[]{:S(2)}, u32[]{:S(2)}) %collective-permute-start.1) | collective-permute-done | bytes 81952 | tf_op jit(solution)/shard_map/ppermute | solution.py:567
  19.8 0.0 copy-done
  19.8 0.0 copy-done.1
  19.8 0.0 copy-done.2
  19.8 6.0 %ghost_pairs.1 = (f32[32,256]{1,0:T(8,128)S(1)}, f32[32,256]{1,0:T(8,128)S(1)}, f32[8,256]{1,0:T(8,128)S(1)}, f32[8,256]{1,0:T(8,128)S(1)}, f32[8,256]{1,0:T(8,128)S(1)}) custom-call(s32[96,128]{1,0:T(8,128)S(1)} %bitcast.12, s32[96,128]{1,0:T(8,128)S(1)} %bitcast.13, s32[96,128]{1,0:T(8,128)S(1)} %bitcast.14, ...), custom_call_target="tpu_custom_call" | custom-call | flops 4915200000 | bytes 147456 | tf_op jit(solution)/shard_map/ghost_pairs/pallas_call | solution.py:687
  25.8 0.3 collective-permute-start.4
  26.1 4.9 %local_pairs.6.refs_4_.refs_7_ = f32[32,256]{1,0:T(8,128)S(1)} custom-call(s32[160,128]{1,0:T(8,128)S(1)} %get-tuple-element.23.refs_0_, f32[72,512]{1,0:T(8,128)S(1)} %get-tuple-element.24.refs_1_.refs_3_, bf16[144,256]{1,0:T(8,128)(2,1)S(1)} %get-tuple-element.25.refs_2_, bf16[1024,256]{1,0:T(8,128)(2,1)S(1)} %get-tuple-element.26.refs_3_.refs_4_, ...), custom_call_target="tpu_custom_call" | custom-call | flops 2048000000 | bytes 61440 | tf_op jit(solution)/shard_map/local_pairs/pallas_call | solution.py:664
  31.0 0.8 %collective-permute-done.4.refs_0_ = f32[32,256]{1,0:T(8,128)S(1)} collective-permute-done((f32[32,256]{1,0:T(8,128)S(1)}, f32[32,256]{1,0:T(8,128)S(1)}, u32[]{:S(2)}, u32[]{:S(2)}) %collective-permute-start.4) | collective-permute-done | bytes 32800 | tf_op jit(solution)/shard_map/ppermute | solution.py:567
  31.8 1.7 %collective-permute-start.5 = (f32[8,256]{1,0:T(8,128)S(1)}, f32[8,256]{1,0:T(8,128)S(1)}, u32[]{:S(2)}, u32[]{:S(2)}) collective-permute-start(f32[8,256]{1,0:T(8,128)S(1)} %get-tuple-element.39), channel_id=1, source_target_pairs={{0,16},{16,0},{1,17},{17,1},{2,18},{18,2},{3,19},{19,3},{4,20},{20... | collective-permute-start | bytes 24584 | tf_op jit(solution)/shard_map/ppermute | solution.py:567
  33.5 0.0 collective-permute-start.6
  33.5 0.9 %collective-permute-start.7 = (f32[8,256]{1,0:T(8,128)S(1)}, f32[8,256]{1,0:T(8,128)S(1)}, u32[]{:S(2)}, u32[]{:S(2)}) collective-permute-start(f32[8,256]{1,0:T(8,128)S(1)} %get-tuple-element.41), channel_id=1, source_target_pairs={{0,20},{4,24},{8,28},{12,16},{16,4},{20,8},{24,12},{28,0},{1,21},{... | collective-permute-start | bytes 24584 | tf_op jit(solution)/shard_map/ppermute | solution.py:567
  34.4 4.3 %local_pairs.7.refs_0_ = f32[32,256]{1,0:T(8,128)S(1)} custom-call(s32[160,128]{1,0:T(8,128)S(1)} %get-tuple-element.23.refs_0_, f32[72,512]{1,0:T(8,128)S(1)} %get-tuple-element.24.refs_1_.refs_3_, bf16[144,256]{1,0:T(8,128)(2,1)S(1)} %get-tuple-element.25.refs_2_, bf16[1024,256]{1,0:T(8,128)(2,1)S(1)} %get-tuple-element.26.refs_3_.refs_4_, ...), custom_call_target="tpu_custom_call" | custom-call | flops 1228800000 | bytes 36864 | tf_op jit(solution)/shard_map/local_pairs/pallas_call | solution.py:664
  38.8 0.0 collective-permute-done.5.refs_3_
  38.8 0.0 collective-permute-done.6.refs_4_
  38.8 0.0 collective-permute-done.7.refs_5_
  38.8 0.8 %totals.1 = (f32[3,512]{1,0:T(4,128)}, f32[1,512]{1,0:T(1,128)}) custom-call(f32[32,256]{1,0:T(8,128)S(1)} %local_pairs.7.refs_0_, s32[1,256]{1,0:T(1,128)S(1)} %get-tuple-element.38.refs_1_, f32[8,256]{1,0:T(8,128)S(1)} %get-tuple-element.37.refs_9_.refs_2_, f32[8,256]{1,0:T(8,128)S(1)} %collective-permute-done.5.refs_3_, ...), custom_call_target="tpu_custom_call" | custom-call | tf_op jit(solution)/shard_map/totals/pallas_call | solution.py:708
  (2 shorter events, 0.0 us)
Async XLA Ops:
  2.5 10.0 %collective-permute-start = (bf16[80,256]{1,0:T(8,128)(2,1)S(1)}, bf16[80,256]{1,0:T(8,128)(2,1)S(1)}, u32[]{:S(2)}, u32[]{:S(2)}) collective-permute-start(bf16[80,256]{1,0:T(8,128)(2,1)S(1)} %get-tuple-element.30.offered_ref), channel_id=1, source_target_pairs={{0,3},{1,0},{2,1},{3,2},{4,7},{5,4},{6,5},{7,6},{8,11},{9,8},{10,9... | collective-permute-start | bytes 122888 | tf_op jit(solution)/shard_map/ppermute | solution.py:567
  12.6 7.3 %copy-start = (s32[12288]{0:T(1024)S(1)}, s32[12288]{0:T(1024)}, u32[]{:S(2)}) copy-start(s32[12288]{0:T(1024)} %param.31) | copy-start | bytes 147460
  12.6 7.2 %copy-start.1 = (s32[12288]{0:T(1024)S(1)}, s32[12288]{0:T(1024)}, u32[]{:S(2)}) copy-start(s32[12288]{0:T(1024)} %param.32) | copy-start | bytes 147460
  12.6 7.2 %copy-start.2 = (s32[12288]{0:T(1024)S(1)}, s32[12288]{0:T(1024)}, u32[]{:S(2)}) copy-start(s32[12288]{0:T(1024)} %param.33) | copy-start | bytes 147460
  12.6 6.8 %collective-permute-start.3 = (bf16[160,256]{1,0:T(8,128)(2,1)S(1)}, bf16[160,256]{1,0:T(8,128)(2,1)S(1)}, u32[]{:S(2)}, u32[]{:S(2)}) collective-permute-start(bf16[160,256]{1,0:T(8,128)(2,1)S(1)} %two_blocks.1.refs_8_), channel_id=1, source_target_pairs={{0,28},{4,16},{8,20},{12,24},{16,12},{20,0},{24,4},{28,8},{1,29},{... | collective-permute-start | bytes 245768 | tf_op jit(solution)/shard_map/ppermute | solution.py:567
  14.3 5.1 %collective-permute-start.2 = (bf16[160,256]{1,0:T(8,128)(2,1)S(1)}, bf16[160,256]{1,0:T(8,128)(2,1)S(1)}, u32[]{:S(2)}, u32[]{:S(2)}) collective-permute-start(bf16[160,256]{1,0:T(8,128)(2,1)S(1)} %two_blocks.1.refs_8_), channel_id=1, source_target_pairs={{0,12},{4,0},{8,4},{12,8},{1,13},{5,1},{9,5},{13,9},{2,14},{6,2},{... | collective-permute-start | bytes 245768 | tf_op jit(solution)/shard_map/ppermute | solution.py:567
  15.4 4.4 %collective-permute-start.1 = (bf16[160,256]{1,0:T(8,128)(2,1)S(1)}, bf16[160,256]{1,0:T(8,128)(2,1)S(1)}, u32[]{:S(2)}, u32[]{:S(2)}) collective-permute-start(bf16[160,256]{1,0:T(8,128)(2,1)S(1)} %two_blocks.1.refs_8_), channel_id=1, source_target_pairs={{0,16},{16,0},{1,17},{17,1},{2,18},{18,2},{3,19},{19,3},{4,20},{20... | collective-permute-start | bytes 245768 | tf_op jit(solution)/shard_map/ppermute | solution.py:567
  25.8 6.0 %collective-permute-start.4 = (f32[32,256]{1,0:T(8,128)S(1)}, f32[32,256]{1,0:T(8,128)S(1)}, u32[]{:S(2)}, u32[]{:S(2)}) collective-permute-start(f32[32,256]{1,0:T(8,128)S(1)} %get-tuple-element.33), channel_id=1, source_target_pairs={{0,1},{1,2},{2,3},{3,0},{4,5},{5,6},{6,7},{7,4},{8,9},{9,10},{10,1... | collective-permute-start | bytes 98312 | tf_op jit(solution)/shard_map/ppermute | solution.py:567
  31.8 7.0 %collective-permute-start.5 = (f32[8,256]{1,0:T(8,128)S(1)}, f32[8,256]{1,0:T(8,128)S(1)}, u32[]{:S(2)}, u32[]{:S(2)}) collective-permute-start(f32[8,256]{1,0:T(8,128)S(1)} %get-tuple-element.39), channel_id=1, source_target_pairs={{0,16},{16,0},{1,17},{17,1},{2,18},{18,2},{3,19},{19,3},{4,20},{20... | collective-permute-start | bytes 24584 | tf_op jit(solution)/shard_map/ppermute | solution.py:567
  33.5 5.3 %collective-permute-start.6 = (f32[8,256]{1,0:T(8,128)S(1)}, f32[8,256]{1,0:T(8,128)S(1)}, u32[]{:S(2)}, u32[]{:S(2)}) collective-permute-start(f32[8,256]{1,0:T(8,128)S(1)} %get-tuple-element.40), channel_id=1, source_target_pairs={{0,4},{4,8},{8,12},{12,0},{1,5},{5,9},{9,13},{13,1},{2,6},{6,10},{... | collective-permute-start | bytes 24584 | tf_op jit(solution)/shard_map/ppermute | solution.py:567
  33.5 5.3 %collective-permute-start.7 = (f32[8,256]{1,0:T(8,128)S(1)}, f32[8,256]{1,0:T(8,128)S(1)}, u32[]{:S(2)}, u32[]{:S(2)}) collective-permute-start(f32[8,256]{1,0:T(8,128)S(1)} %get-tuple-element.41), channel_id=1, source_target_pairs={{0,20},{4,24},{8,28},{12,16},{16,4},{20,8},{24,12},{28,0},{1,21},{... | collective-permute-start | bytes 24584 | tf_op jit(solution)/shard_map/ppermute | solution.py:567
